TPU v7x, 256 devices: a whole 4x4x8 slice. The times are simulated.
256 devices in a mesh: ep: 32 (over x, y, core), etp: 8 (over z).
Axes of the slice: x: 4, y: 4, z: 8, core: 2. Of those that a mesh axis runs over, the one named last changes fastest.
Arguments:
- tokens: bfloat16 [4096, 3584], P('ep'), may hold values from -6 to 6
- out_grad: bfloat16 [4096, 3584], P('ep'), may hold values from -6 to 6
- expert_ids: int32 [4096, 2], P('ep'), may hold values from 0 to 31, as said below
- route_probs: bfloat16 [4096, 2], P('ep'), may hold values from 0.099609375 to 1
- w_gate: bfloat16 [32, 3584, 3200], P('ep', None, 'etp'), may hold values from -0.09375 to 0.09375
- w_up: bfloat16 [32, 3584, 3200], P('ep', None, 'etp'), may hold values from -0.09375 to 0.09375
- w_down: bfloat16 [32, 3200, 3584], P('ep', 'etp'), may hold values from -0.109375 to 0.109375
Outputs:
- token_grad: bfloat16 [4096, 3584], P('ep')
- prob_grad: bfloat16 [4096, 2], P('ep')
- down_grad: bfloat16 [32, 3200, 3584], P('ep', 'etp')
Inputs may be any that keep to these rules, and one draw needn't show every extreme that they name: `expert_ids`: each row names two different experts. Among the 128 rows of one device (aligned blocks of rows) no expert is named more than 16 times, and in every draw one expert is named exactly 16 times within the rows of every device.
All inputs are finite; a program needn't handle non-finite values.
Results may differ from a plain program's by a relative error of at most 0.02.
Values may be sent and summed in bfloat16 or wider, within the bound.
No kernel may reach another device: no remote copies, remote signals or barrier semaphores. Data moves between devices by JAX's collectives and lax.ppermute only.
A program may use at most 128 MiB of HBM per device.

v0:
```python
import jax
import jax.numpy as jnp
from jax import lax
from jax.sharding import PartitionSpec as P


def contract_last(left, right):
    return lax.dot_general(
        left, right, (((1,), (1,)), ((), ())), preferred_element_type=jnp.float32
    )


def on_device(tokens, out_grad, expert_ids, route_probs, w_gate, w_up, w_down):
    tok_rows = tokens.shape[0]
    features = tokens.shape[1]
    experts = lax.axis_size("ep")
    capacity = 4 * tok_rows // experts
    slot_rows = experts * capacity
    flat_ids = expert_ids.T.reshape(-1)
    flat_probs = route_probs.T.reshape(-1)
    one_hot = (flat_ids[:, None] == jnp.arange(experts, dtype=jnp.int32)[None, :]).astype(jnp.int32)
    position = jnp.sum((jnp.cumsum(one_hot, axis=0) - 1) * one_hot, axis=1)
    slot_of = flat_ids * capacity + position
    source = (
        jnp.zeros((slot_rows,), jnp.int32)
        .at[slot_of]
        .set(jnp.arange(2 * tok_rows, dtype=jnp.int32) + 1)
    )
    filled = source > 0
    route_index = jnp.maximum(source - 1, 0)
    token_of = route_index % tok_rows
    send_probs = jnp.where(filled, flat_probs[route_index], 0).reshape(experts, capacity)
    send_tokens = jnp.where(filled[:, None], tokens[token_of], 0).reshape(
        experts, capacity, features
    )
    send_grad = jnp.where(filled[:, None], out_grad[token_of], 0).reshape(
        experts, capacity, features
    )
    got_tokens, got_grad, got_probs = (
        lax.all_to_all(send_tokens, "ep", split_axis=0, concat_axis=0, tiled=True),
        lax.all_to_all(send_grad, "ep", split_axis=0, concat_axis=0, tiled=True),
        lax.all_to_all(send_probs, "ep", split_axis=0, concat_axis=0, tiled=True),
    )
    token_rows = got_tokens.reshape(slot_rows, features)
    grad_rows = got_grad.reshape(slot_rows, features)
    prob_rows = got_probs.reshape(slot_rows).astype(jnp.float32)
    gate_matrix = w_gate[0]
    up_matrix = w_up[0]
    down_matrix = w_down[0]
    gate_value = jnp.dot(token_rows, gate_matrix, preferred_element_type=jnp.float32)
    up_value = jnp.dot(token_rows, up_matrix, preferred_element_type=jnp.float32)
    gate_sigmoid = jax.nn.sigmoid(gate_value)
    hidden = (gate_value * gate_sigmoid * up_value).astype(jnp.bfloat16)
    hidden_grad = contract_last(grad_rows, down_matrix)
    scaled_back = prob_rows[:, None] * hidden_grad
    up_grad = (scaled_back * gate_value * gate_sigmoid).astype(jnp.bfloat16)
    gate_grad = (
        scaled_back * up_value * gate_sigmoid * (1.0 + gate_value * (1.0 - gate_sigmoid))
    ).astype(jnp.bfloat16)
    partial_value = contract_last(gate_grad, gate_matrix) + contract_last(up_grad, up_matrix)
    score_part = jnp.sum(hidden_grad * hidden.astype(jnp.float32), axis=1)
    weighted_grad = (prob_rows[:, None] * grad_rows).astype(jnp.bfloat16)
    down_local = lax.dot_general(
        hidden, weighted_grad, (((0,), (0,)), ((), ())), preferred_element_type=jnp.float32
    )
    down_grad = down_local.astype(jnp.bfloat16)[None]
    summed, score_total = (
        lax.psum(partial_value.astype(jnp.bfloat16), "etp").astype(jnp.float32),
        lax.psum(score_part.astype(jnp.bfloat16), "etp").astype(jnp.float32),
    )
    back_rows = summed.astype(jnp.bfloat16).reshape(experts, capacity, features)
    back_score = score_total.astype(jnp.bfloat16).reshape(experts, capacity)
    returned, returned_score = (
        lax.all_to_all(back_rows, "ep", split_axis=0, concat_axis=0, tiled=True),
        lax.all_to_all(back_score, "ep", split_axis=0, concat_axis=0, tiled=True),
    )
    route_grad = returned.reshape(slot_rows, features)[slot_of]
    token_grad = (
        route_grad[:tok_rows].astype(jnp.float32) + route_grad[tok_rows:].astype(jnp.float32)
    ).astype(jnp.bfloat16)
    prob_grad = returned_score.reshape(slot_rows)[slot_of].reshape(2, tok_rows).T
    return (token_grad, prob_grad, down_grad)


def solution(mesh):
    return jax.shard_map(
        on_device,
        mesh=mesh,
        in_specs=(
            P("ep", None),
            P("ep", None),
            P("ep", None),
            P("ep", None),
            P("ep", None, "etp"),
            P("ep", None, "etp"),
            P("ep", "etp", None),
        ),
        out_specs=(P("ep", None), P("ep", None), P("ep", "etp", None)),
        check_vma=False,
    )
```

profile of v0, /device:TPU:32, one launch (start us, length us, event | category | flops | bytes accessed | tf_op | source)
XLA Modules:
  0.0 332.5 jit_solution(14338923412853324280)
XLA Ops:
  7.2 0.8 broadcast_multiply_fusion
  8.0 0.7 fusion.17
  8.7 0.6 reduce-window.6
  9.3 0.2 slice_reduce_fusion
  9.5 0.8 fusion.16
  10.3 1.4 scatter_custom_fusion
  11.8 3.5 %gather_fusion = bf16[512]{0:T(512)(128)(2,1)S(1)} fusion(bf16[256]{0:T(256)(128)(2,1)} %bitcast.55, s32[1024]{0:T(1024)S(1)} %get-tuple-element.13), kind=kCustom, calls=%fused_computation | custom fusion | bytes 4096 | tf_op jit(solution)/shard_map/gather | solution.py:32
  15.2 0.7 all_to_all.28
  15.9 7.3 %all-to-all-start = ((bf16[32,1,16]{2,1,0:T(2,128)(2,1)}), bf16[32,1,16]{2,1,0:T(2,128)(2,1)S(1)}, u32[]{:S(2)}, u32[]{:S(2)}) async-start(bf16[32,1,16]{2,1,0:T(2,128)(2,1)} %all_to_all.28), calls=%async_computation | async-start | bytes 32768 | tf_op jit(solution)/shard_map/all_to_all | solution.py:42
  23.3 0.1 broadcast_in_dim.42
  23.4 9.2 %gather_fusion.2 = bf16[512,3584]{1,0:T(8,128)(2,1)} fusion(bf16[128,3584]{1,0:T(8,128)(2,1)} %param.7, s32[1024]{0:T(1024)S(1)} %get-tuple-element.12), kind=kCustom, calls=%fused_computation.2 | custom fusion | bytes 7342080 | tf_op jit(solution)/shard_map/gather | solution.py:33
  32.6 9.2 %gather_fusion.1 = bf16[512,3584]{1,0:T(8,128)(2,1)} fusion(bf16[128,3584]{1,0:T(8,128)(2,1)} %param.8, s32[1024]{0:T(1024)S(1)} %get-tuple-element.12), kind=kCustom, calls=%fused_computation.1 | custom fusion | bytes 7342080 | tf_op jit(solution)/shard_map/gather | solution.py:36
  41.8 5.3 %broadcast_select_fusion.1 = (bf16[32,16,3584]{2,1,0:T(8,128)(2,1)}, bf16[32,16,3584]{2,1,0:T(8,128)(2,1)}) fusion(bf16[32,16,3584]{2,1,0:T(8,128)(2,1)} %bitcast.57, pred[32,16]{1,0:T(8,128)(4,1)S(1)} %broadcast_in_dim.42, bf16[32,16,3584]{2,1,0:T(8,128)(2,1)} %bitcast.56), kind=kLoop, calls=%fused_computation.12 | loop fusion | flops 3670016 | bytes 14680576 | tf_op jit(solution)/shard_map/jit(_where)/select_n | solution.py:36
  47.0 52.3 %all_to_all.34 = bf16[32,16,3584]{2,1,0:T(8,128)(2,1)} all-to-all(bf16[32,16,3584]{2,1,0:T(8,128)(2,1)} %get-tuple-element.8), channel_id=1, replica_groups=mesh['ep'=32,'etp'=8] {'ep'}, dimensions={0} | all-to-all | bytes 7340032 | tf_op jit(solution)/shard_map/all_to_all | solution.py:40
  99.4 4.8 %all-to-all-start.1 = ((bf16[32,16,3584]{2,1,0:T(8,128)(2,1)}), bf16[32,16,3584]{2,1,0:T(8,128)(2,1)}, u32[]{:S(2)}, u32[]{:S(2)}) async-start(bf16[32,16,3584]{2,1,0:T(8,128)(2,1)} %get-tuple-element.7), calls=%async_computation.1 | async-start | bytes 7340032 | tf_op jit(solution)/shard_map/all_to_all | solution.py:41
  104.2 0.2 all-reduce.2.cloned.1.call-start
  104.6 4.8 %fusion.4 = f32[512,400]{0,1:T(8,128)} fusion(bf16[512,3584]{1,0:T(8,128)(2,1)} %bitcast.59, bf16[1,3584,400]{1,2,0:T(8,128)(2,1)S(1)} %copy-done), kind=kOutput, calls=%fused_computation.15 | convolution fusion | flops 1468006400 | bytes 7356416 | tf_op jit(solution)/shard_map/dot_general | solution.py:50
  109.4 2.6 fusion.7
  111.9 39.0 %all-to-all-done.1 = bf16[32,16,3584]{2,1,0:T(8,128)(2,1)} async-done(((bf16[32,16,3584]{2,1,0:T(8,128)(2,1)}), bf16[32,16,3584]{2,1,0:T(8,128)(2,1)}, u32[]{:S(2)}, u32[]{:S(2)}) %all-to-all-start.1) | async-done | bytes 3670048 | tf_op jit(solution)/shard_map/all_to_all | solution.py:41
  150.9 5.2 %multiply_reduce_fusion = (bf16[512]{0:T(512)(128)(2,1)S(1)}, bf16[512,400]{0,1:T(8,128)(2,1)S(1)}, f32[512,400]{0,1:T(8,128)S(1)}) fusion(f32[512,400]{0,1:T(8,128)} %fusion.7, f32[512,400]{0,1:T(8,128)} %fusion.4, bf16[512,3584]{1,0:T(8,128)(2,1)} %bitcast.9, bf16[1,400,3584]{2,1,0:T(8,128)(2,1)} %param.13), kind=kOutput, calls=%fused_computation.23 | convolution fusion | flops 1469849088 | bytes 9405440 | tf_op jit(solution)/shard_map/dot_general | solution.py:8
  156.1 2.2 fusion.2
  158.4 4.2 %add_convert_fusion = bf16[512,3584]{1,0:T(8,128)(2,1)} fusion(f32[512,3584]{1,0:T(8,128)S(1)} %fusion.2, bf16[1,3584,400]{1,2,0:T(8,128)(2,1)S(1)} %copy-done.5, f32[512,400]{0,1:T(8,128)S(1)} %copy-done.2, f32[512,400]{0,1:T(8,128)S(1)} %get-tuple-element.11, f32[512]{0:T(512)S(1)} %reshape.115), kind=kOutput, calls=%fused_computation.7 | convolution fusion | flops 1473110016 | bytes 15517696 | tf_op jit(solution)/shard_map/dot_general | solution.py:8
  162.7 18.1 %psum.15 = bf16[32,1,16]{2,0,1:T(8,128)(2,1)S(1)} all-reduce(bf16[32,1,16]{2,0,1:T(8,128)(2,1)S(1)} %all_to_all.26), channel_id=1, replica_groups=mesh['ep'=32,'etp'=8] {'etp'}, use_global_device_ids=true, to_apply=%region_6.7 | all-reduce | flops 512 | bytes 2048 | tf_op jit(solution)/shard_map/psum | solution.py:69
  180.9 13.3 %all_to_all.35 = bf16[32,1,16]{2,1,0:T(2,128)(2,1)S(1)} all-to-all(bf16[32,1,16]{2,1,0:T(2,128)(2,1)S(1)} %copy.13), channel_id=1, replica_groups=mesh['ep'=32,'etp'=8] {'ep'}, dimensions={0} | all-to-all | bytes 2048 | tf_op jit(solution)/shard_map/all_to_all | solution.py:75
  194.2 67.9 %all-reduce.2.cloned.1.call-done = bf16[32,16,3584]{2,1,0:T(8,128)(2,1)} async-done(((bf16[32,16,3584]{2,1,0:T(8,128)(2,1)}), bf16[32,16,3584]{2,1,0:T(8,128)(2,1)}) %all-reduce.2.cloned.1.call-update) | async-done | bytes 3670032 | tf_op jit(solution)/shard_map/psum | solution.py:68
  262.0 7.4 %all-to-all-start.3 = ((bf16[32,16,3584]{2,1,0:T(8,128)(2,1)}), bf16[32,16,3584]{2,1,0:T(8,128)(2,1)}, u32[]{:S(2)}, u32[]{:S(2)}) async-start(bf16[32,16,3584]{2,1,0:T(8,128)(2,1)} %all-reduce.2.cloned.1.call-done), calls=%async_computation.3 | async-start | bytes 7340032 | tf_op jit(solution)/shard_map/all_to_all | solution.py:74
  269.5 5.4 %fusion = bf16[1,400,3584]{2,1,0:T(8,128)(2,1)} fusion(bf16[512,400]{0,1:T(8,128)(2,1)S(1)} %get-tuple-element.4, bf16[512,3584]{1,0:T(8,128)(2,1)} %bitcast.9, f32[512]{0:T(512)S(1)} %reshape.115), kind=kOutput, calls=%fused_computation.9 | convolution fusion | flops 1474945024 | bytes 6948864 | tf_op jit(solution)/shard_map/dot_general | solution.py:63
  274.9 0.1 reshape.113
  275.0 2.4 gather_fusion.4
  277.4 38.3 %all-to-all-done.3 = bf16[32,16,3584]{2,1,0:T(8,128)(2,1)} async-done(((bf16[32,16,3584]{2,1,0:T(8,128)(2,1)}), bf16[32,16,3584]{2,1,0:T(8,128)(2,1)}, u32[]{:S(2)}, u32[]{:S(2)}) %all-to-all-start.3) | async-done | bytes 3670048 | tf_op jit(solution)/shard_map/all_to_all | solution.py:74
  315.7 7.3 %gather_fusion.3 = bf16[256,3584]{1,0:T(8,128)(2,1)} fusion(bf16[512,3584]{1,0:T(8,128)(2,1)} %bitcast.16, s32[1024]{0:T(1024)S(1)} %pad_clamp_fusion), kind=kCustom, calls=%fused_computation.3 | custom fusion | bytes 3671040 | tf_op jit(solution)/shard_map/gather | solution.py:77
  323.0 2.6 add_convert_fusion.1
  (27 shorter events, 0.4 us)
Async XLA Ops:
  7.2 97.4 %copy-start = (bf16[1,3584,400]{1,2,0:T(8,128)(2,1)S(1)}, bf16[1,3584,400]{1,2,0:T(8,128)(2,1)}, u32[]{:S(2)}) copy-start(bf16[1,3584,400]{1,2,0:T(8,128)(2,1)} %param.11) | copy-start | bytes 8601604
  15.9 31.1 %all-to-all-start = ((bf16[32,1,16]{2,1,0:T(2,128)(2,1)}), bf16[32,1,16]{2,1,0:T(2,128)(2,1)S(1)}, u32[]{:S(2)}, u32[]{:S(2)}) async-start(bf16[32,1,16]{2,1,0:T(2,128)(2,1)} %all_to_all.28), calls=%async_computation | async-start | bytes 32768 | tf_op jit(solution)/shard_map/all_to_all | solution.py:42
  99.4 51.5 %all-to-all-start.1 = ((bf16[32,16,3584]{2,1,0:T(8,128)(2,1)}), bf16[32,16,3584]{2,1,0:T(8,128)(2,1)}, u32[]{:S(2)}, u32[]{:S(2)}) async-start(bf16[32,16,3584]{2,1,0:T(8,128)(2,1)} %get-tuple-element.7), calls=%async_computation.1 | async-start | bytes 7340032 | tf_op jit(solution)/shard_map/all_to_all | solution.py:41
  104.2 157.8 %all-reduce.2.cloned.1.call-start = ((), (), s32[]{:S(2)}) async-start(), calls=%async_computation.5 | async-start | bytes 7340032 | tf_op jit(solution)/shard_map/psum | solution.py:68
  104.6 4.8 %copy-start.1 = (bf16[32,16,3584]{2,1,0:T(8,128)(2,1)S(1)}, bf16[32,16,3584]{2,1,0:T(8,128)(2,1)}, u32[]{:S(2)}) copy-start(bf16[32,16,3584]{2,1,0:T(8,128)(2,1)} %all_to_all.34) | copy-start | bytes 11010052
  104.6 4.8 %copy-start.4 = (bf16[1,3584,400]{1,2,0:T(8,128)(2,1)S(1)}, bf16[1,3584,400]{1,2,0:T(8,128)(2,1)}, u32[]{:S(2)}) copy-start(bf16[1,3584,400]{1,2,0:T(8,128)(2,1)} %param.12) | copy-start | bytes 8601604
  150.9 5.2 %copy-start.2 = (f32[512,400]{0,1:T(8,128)S(1)}, f32[512,400]{0,1:T(8,128)}, u32[]{:S(2)}) copy-start(f32[512,400]{0,1:T(8,128)} %fusion.4) | copy-start | bytes 2457604
  150.9 5.2 %copy-start.3 = (f32[512,400]{0,1:T(8,128)S(1)}, f32[512,400]{0,1:T(8,128)}, u32[]{:S(2)}) copy-start(f32[512,400]{0,1:T(8,128)} %fusion.7) | copy-start | bytes 2457604
  156.1 2.3 copy-start.5
  262.0 53.7 %all-to-all-start.3 = ((bf16[32,16,3584]{2,1,0:T(8,128)(2,1)}), bf16[32,16,3584]{2,1,0:T(8,128)(2,1)}, u32[]{:S(2)}, u32[]{:S(2)}) async-start(bf16[32,16,3584]{2,1,0:T(8,128)(2,1)} %all-reduce.2.cloned.1.call-done), calls=%async_computation.3 | async-start | bytes 7340032 | tf_op jit(solution)/shard_map/all_to_all | solution.py:74
Sparse Core Ops, SparseCore 0:
  162.7 99.2 all-reduce.1
where the time goes:
time: 336 us; the launch traced here: 332 us
  waiting for transfers between devices  145 us (43%)
  blocking collectives  83.8 us (25%)
  local copies, waits for them, and re-layouts  34.3 us (10%)
  matrix products  24.3 us (7%)
  starting transfers between devices  19.8 us (6%)
  between operations  14.2 us (4%)
  other arithmetic  10.9 us (3%)
    psum x1, waiting for transfers between devices, on_device(): lax.psum(partial_value.astype(jnp.bfloat16), 'etp').astype(jnp.float32)  67.9 us
    all_to_all x1, blocking collectives, on_device(): lax.all_to_all(send_tokens, 'ep', split_axis=0, concat_axis=0, tiled=True)  52.3 us
    all_to_all x1, waiting for transfers between devices, on_device(): lax.all_to_all(send_grad, 'ep', split_axis=0, concat_axis=0, tiled=True)  39 us
    all_to_all x1, waiting for transfers between devices, on_device(): lax.all_to_all(back_rows, 'ep', split_axis=0, concat_axis=0, tiled=True)  38.3 us
    psum x1, blocking collectives, on_device(): lax.psum(score_part.astype(jnp.bfloat16), 'etp').astype(jnp.float32)  18.1 us
    all_to_all x1, blocking collectives, on_device(): lax.all_to_all(back_score, 'ep', split_axis=0, concat_axis=0, tiled=True)  13.3 us
    dot_general x3, matrix products, contract_last(): lax.dot_general(left, right, (((1,), (1,)), ((), ())), preferred_element_...  11.7 us
    gather x1, local copies, waits for them, and re-layouts, on_device(): tokens[token_of]  9.22 us
  transfers between devices with their start and end apart: 4, of which 3 were waited for; matrix products, arithmetic and copies ran while one was open for 12% of the time, Pallas kernels for 0%

commit v1 on v0

v1 whole, which is shorter than its diff:
```python
import functools

import jax
import jax.numpy as jnp
from jax import lax
from jax.experimental import pallas as pl
from jax.experimental.pallas import tpu as pltpu
from jax.sharding import PartitionSpec as P

D = 3584
UNITS = 400
TOK = 128
EXPERTS = 32
N_Z = 8
ROWS = 256
QUARTER = D // 4
WIDE = 384
PACK = 2 * WIDE + 128
BF = jnp.bfloat16
F32 = jnp.float32
VMEM_BYTES = 56 * 2**20

NT = (((1,), (1,)), ((), ()))
TN = (((0,), (0,)), ((), ()))
NN = (((1,), (0,)), ((), ()))


def mm(left, right, dims=NN):
    return lax.dot_general(left, right, dims, preferred_element_type=F32)


def params():
    return pltpu.CompilerParams(vmem_limit_bytes=VMEM_BYTES)


VM = pl.BlockSpec(memory_space=pltpu.VMEM)
SM = pl.BlockSpec(memory_space=pltpu.SMEM)
ANY = pl.BlockSpec(memory_space=pl.ANY)


def slots_of(ids_ref):
    expert = lax.broadcasted_iota(jnp.int32, (EXPERTS, TOK), 0)
    first = ids_ref[0:1, :]
    second = ids_ref[1:2, :]
    hot0 = (expert == first).astype(F32)
    hot1 = (expert == second).astype(F32)
    earlier = lax.broadcasted_iota(jnp.int32, (TOK, TOK), 0) < lax.broadcasted_iota(
        jnp.int32, (TOK, TOK), 1
    )
    before = earlier.astype(BF)
    rank0 = mm(hot0.astype(BF), before)
    rank1 = mm(hot1.astype(BF), before) + jnp.sum(hot0, axis=1, keepdims=True)
    pos0 = jnp.sum(hot0 * rank0, axis=0, keepdims=True).astype(jnp.int32)
    pos1 = jnp.sum(hot1 * rank1, axis=0, keepdims=True).astype(jnp.int32)
    return first * 16 + pos0, second * 16 + pos1


def row_hot(slot, half):
    row = lax.broadcasted_iota(jnp.int32, (ROWS, TOK), 0)
    return ((row >> 3) * 16 + half * 8 + (row & 7)) == slot


def send_tokens_kernel(z_ref, ids_ref, tok_ref, out_ref):
    z = z_ref[0]
    slot0, slot1 = slots_of(ids_ref)
    half = z // 4
    hot = jnp.logical_or(row_hot(slot0, half), row_hot(slot1, half)).astype(BF)
    cols = pl.ds(pl.multiple_of((z % 4) * QUARTER, 128), QUARTER)
    out_ref[...] = mm(hot, tok_ref[:, cols]).astype(BF)


def send_grads_kernel(ids_ref, prob_ref, grad_ref, out0_ref, out1_ref):
    slot0, slot1 = slots_of(ids_ref)
    p0 = prob_ref[0:1, :].astype(F32)
    p1 = prob_ref[1:2, :].astype(F32)
    for half, out_ref in ((0, out0_ref), (1, out1_ref)):
        hot0 = row_hot(slot0, half)
        hot1 = row_hot(slot1, half)
        hot = jnp.logical_or(hot0, hot1).astype(BF)
        prob = jnp.sum(
            jnp.where(hot0, p0, 0.0) + jnp.where(hot1, p1, 0.0), axis=1, keepdims=True
        )
        for c in range(0, D, QUARTER):
            out_ref[:, c : c + QUARTER] = (
                mm(hot, grad_ref[:, c : c + QUARTER]) * prob
            ).astype(BF)


def gate_up_kernel(offsets, z_ref, *refs):
    xs = refs[:8]
    gate_w, up_w = refs[8:10]
    outs = refs[10:14]
    x_buf, wg_buf, wu_buf, sems = refs[14:]
    z = z_ref[0]
    copies = [
        pltpu.make_async_copy(gate_w, wg_buf, sems.at[8]),
        pltpu.make_async_copy(up_w, wu_buf, sems.at[9]),
    ]
    for i, off in enumerate(offsets):
        owner = lax.rem(z + off + 8, 8)
        cols = pl.ds(pl.multiple_of(lax.rem(owner, 4) * QUARTER, 128), QUARTER)
        copies.append(
            pltpu.make_async_copy(xs[i], x_buf.at[owner // 4, :, cols], sems.at[i])
        )
    for c in copies:
        c.start()
    for c in copies:
        c.wait()
    for half in range(2):
        outs[2 * half][...] = mm(x_buf[half], wg_buf[...], NT)
        outs[2 * half + 1][...] = mm(x_buf[half], wu_buf[...], NT)


def expert_kernel(
    z_ref, rows_hbm, down_w, gate_w, up_w, gate_ref, up_ref, *refs
):
    packs = refs[:8]
    score_ref, hid_ref, rows, wd, wg, wu, part, sems = refs[8:]
    z = z_ref[0]
    c_rows = pltpu.make_async_copy(rows_hbm, rows, sems.at[0])
    c_wd = pltpu.make_async_copy(down_w, wd, sems.at[1])
    c_wg = pltpu.make_async_copy(gate_w, wg, sems.at[2])
    c_wu = pltpu.make_async_copy(up_w, wu, sems.at[3])
    for c in (c_rows, c_wd, c_wg, c_wu):
        c.start()
    c_rows.wait()
    c_wd.wait()
    back = mm(rows[...], wd[...], NT)
    gate = gate_ref[...]
    up = up_ref[...]
    sig = jax.nn.sigmoid(gate)
    hidden = (gate * sig * up).astype(BF)
    hid_ref[...] = hidden
    up_grad = (back * gate * sig).astype(BF)
    gate_grad = (back * up * sig * (1.0 + gate * (1.0 - sig))).astype(BF)
    score = jnp.sum(back * hidden.astype(F32), axis=1, keepdims=True)
    score_ref[...] = jnp.broadcast_to(score, (ROWS, 128)).astype(BF)
    c_wg.wait()
    c_wu.wait()
    for c in range(0, D, QUARTER):
        part[:, c : c + QUARTER] = (
            mm(gate_grad, wg[:, c : c + QUARTER]) + mm(up_grad, wu[:, c : c + QUARTER])
        ).astype(BF)
    lane = lax.broadcasted_iota(jnp.int32, (128, 128), 1)
    for r in range(8):
        shard = lax.rem(z + r, 8)
        cols = pl.ds(pl.multiple_of(shard * WIDE, 128), WIDE)
        tile = pl.ds(pl.multiple_of((24 + shard // 2) * 128, 128), 128)
        packs[r][:, :WIDE] = part[0:128, cols]
        packs[r][:, WIDE : 2 * WIDE] = part[128:256, cols]
        top = part[0:128, tile].astype(F32)
        bottom = part[128:256, tile].astype(F32)
        odd = lax.rem(shard, 2) == 1
        top = jnp.where(odd, pltpu.roll(top, 64, 1), top)
        bottom = jnp.where(odd, bottom, pltpu.roll(bottom, 64, 1))
        packs[r][:, 2 * WIDE :] = jnp.where(lane < 64, top, bottom).astype(BF)


def back_kernel(*refs):
    out_ref = refs[8]
    lane = lax.broadcasted_iota(jnp.int32, (128, 128), 1)
    tiles = []
    for half in range(2):
        own, left, right = refs[3 * half : 3 * half + 3]
        total = (
            own[...].astype(F32) + left[...].astype(F32) + right[...].astype(F32)
        )
        base = half * WIDE
        out_ref[0:128, base : base + WIDE] = total[:, :WIDE].astype(BF)
        out_ref[128:256, base : base + WIDE] = total[:, WIDE : 2 * WIDE].astype(BF)
        tile = total[:, 2 * WIDE :]
        tiles.append((tile, pltpu.roll(tile, 64, 1)))
    (t0, r0), (t1, r1) = tiles
    out_ref[0:128, 2 * WIDE : PACK] = jnp.where(lane < 64, t0, r1).astype(BF)
    out_ref[128:256, 2 * WIDE : PACK] = jnp.where(lane < 64, r0, t1).astype(BF)
    score0, score1 = refs[6], refs[7]
    wide = lax.broadcasted_iota(jnp.int32, (ROWS, 128), 1)
    out_ref[:, PACK:] = jnp.where(
        wide == 0, score0[...].astype(F32), jnp.where(wide == 1, score1[...].astype(F32), 0.0)
    ).astype(BF)


def token_sum_kernel(ids_ref, got_ref, out_ref):
    slot0, slot1 = slots_of(ids_ref)
    hots = [
        [row_hot(slot, half).astype(BF) for slot in (slot0, slot1)] for half in range(2)
    ]
    both = [h[0] + h[1] for h in hots]
    out_ref[:, :WIDE] = (
        mm(both[0], got_ref[:, :WIDE], TN) + mm(both[1], got_ref[:, WIDE : 2 * WIDE], TN)
    ).astype(BF)
    tile = got_ref[:, 2 * WIDE : PACK]
    low = mm(both[0], tile, TN)
    high = pltpu.roll(mm(both[1], tile, TN), 64, 1)
    scores = got_ref[:, PACK:]
    lane = lax.broadcasted_iota(jnp.int32, (128, 128), 1)
    result = jnp.where(lane < 64, low + high, 0.0)
    for k in range(2):
        total = mm(hots[0][k], scores, TN)[:, 0:1] + mm(hots[1][k], scores, TN)[:, 1:2]
        result = jnp.where(lane == 64 + k, total, result)
    out_ref[:, WIDE:] = result.astype(BF)


def assemble_kernel(offsets, z_ref, *refs):
    shards = refs[:8]
    out_ref, prob_ref, tiles = refs[8:]
    z = z_ref[0]
    total = jnp.zeros((128, 128), F32)
    for i, off in enumerate(offsets):
        owner = lax.rem(z + off + 8, 8)
        cols = pl.ds(pl.multiple_of(owner * WIDE, 128), WIDE)
        out_ref[:, cols] = shards[i][:, :WIDE]
        tile = shards[i][:, WIDE:].astype(F32)
        tiles[owner] = tile
        total = total + tile
    prob_ref[...] = total
    lane = lax.broadcasted_iota(jnp.int32, (128, 128), 1)
    for j in range(4):
        c = 8 * WIDE + 128 * j
        out_ref[:, c : c + 128] = jnp.where(
            lane < 64, tiles[2 * j], pltpu.roll(tiles[2 * j + 1], 64, 1)
        ).astype(BF)


def down_kernel(hid0, hid1, rows0, rows1, out_ref):
    out_ref[...] = (
        mm(hid0[...], rows0[...], TN) + mm(hid1[...], rows1[...], TN)
    ).astype(BF)


RIGHT = [(i, (i + 1) % N_Z) for i in range(N_Z)]
LEFT = [(i, (i - 1) % N_Z) for i in range(N_Z)]
OFFSETS = (0, -1, 1, -2, 2, -3, 3, -4)


def to_right(x):
    return lax.ppermute(x, "etp", RIGHT)


def to_left(x):
    return lax.ppermute(x, "etp", LEFT)


def ring_gather(x):
    shards = [x]
    from_left = from_right = x
    for step in range(4):
        from_left = to_right(from_left)
        shards.append(from_left)
        if step < 3:
            from_right = to_left(from_right)
            shards.append(from_right)
    return shards


def add_rows(a, b):
    return (a.astype(F32) + b.astype(F32)).astype(BF)


def ring_scatter(packs):
    from_left = to_right(packs[4])
    from_right = to_left(packs[5])
    for step in range(3):
        from_left = to_right(add_rows(from_left, packs[3 - step]))
        if step < 2:
            from_right = to_left(add_rows(from_right, packs[6 + step]))
    return from_left, from_right


def exchange(x):
    return lax.all_to_all(x, "ep", split_axis=0, concat_axis=0, tiled=True)


def shape(*dims, dtype=BF):
    return jax.ShapeDtypeStruct(dims, dtype)


def on_device(tokens, out_grad, expert_ids, route_probs, w_gate, w_up, w_down):
    z = lax.axis_index("etp").astype(jnp.int32).reshape(1)
    ids = expert_ids.T
    probs = route_probs.T
    gate_w = w_gate[0].T
    up_w = w_up[0].T
    down_w = w_down[0]

    send_x = pl.pallas_call(
        send_tokens_kernel,
        out_shape=shape(ROWS, QUARTER),
        in_specs=[SM, VM, VM],
        out_specs=VM,
        compiler_params=params(),
        name="send_tokens",
    )(z, ids, tokens)
    got_x = exchange(send_x.reshape(EXPERTS, 8, QUARTER)).reshape(ROWS, QUARTER)
    send_g = pl.pallas_call(
        send_grads_kernel,
        out_shape=[shape(ROWS, D)] * 2,
        in_specs=[VM] * 3,
        out_specs=[VM] * 2,
        compiler_params=params(),
        name="send_grads",
    )(ids, probs, out_grad)
    rows = [exchange(g.reshape(EXPERTS, 8, D)).reshape(ROWS, D) for g in send_g]

    gate_up = pl.pallas_call(
        functools.partial(gate_up_kernel, OFFSETS),
        out_shape=[shape(ROWS, UNITS, dtype=F32)] * 4,
        in_specs=[SM] + [ANY] * 10,
        out_specs=[VM] * 4,
        scratch_shapes=[
            pltpu.VMEM((2, ROWS, D), BF),
            pltpu.VMEM((UNITS, D), BF),
            pltpu.VMEM((UNITS, D), BF),
            pltpu.SemaphoreType.DMA((10,)),
        ],
        compiler_params=params(),
        name="gate_up",
    )(z, *ring_gather(got_x), gate_w, up_w)

    back_parts = []
    scores = []
    hiddens = []
    for half in range(2):
        *packs, score, hidden = pl.pallas_call(
            expert_kernel,
            out_shape=[shape(128, PACK)] * 8 + [shape(ROWS, 128), shape(ROWS, UNITS)],
            in_specs=[SM] + [ANY] * 4 + [VM] * 2,
            out_specs=[VM] * 10,
            scratch_shapes=[
                pltpu.VMEM((ROWS, D), BF),
                pltpu.VMEM((UNITS, D), BF),
                pltpu.VMEM((UNITS, D), BF),
                pltpu.VMEM((UNITS, D), BF),
                pltpu.VMEM((ROWS, D), BF),
                pltpu.SemaphoreType.DMA((4,)),
            ],
            compiler_params=params(),
            name="expert",
        )(z, rows[half], down_w, gate_w, up_w, *gate_up[2 * half : 2 * half + 2])
        back_parts += [packs[0], *ring_scatter(packs)]
        scores.append(score)
        hiddens.append(hidden)

    send_back = pl.pallas_call(
        back_kernel,
        out_shape=shape(ROWS, PACK + 128),
        in_specs=[VM] * 8,
        out_specs=VM,
        compiler_params=params(),
        name="pack_back",
    )(*back_parts, *scores)
    got_back = exchange(send_back.reshape(EXPERTS, 8, PACK + 128)).reshape(ROWS, PACK + 128)
    summed = pl.pallas_call(
        token_sum_kernel,
        out_shape=shape(TOK, 512),
        in_specs=[VM] * 2,
        out_specs=VM,
        compiler_params=params(),
        name="token_sum",
    )(ids, got_back)
    token_grad, prob_total = pl.pallas_call(
        functools.partial(assemble_kernel, OFFSETS),
        out_shape=[shape(TOK, D), shape(128, 128, dtype=F32)],
        in_specs=[SM] + [VM] * 8,
        out_specs=[VM] * 2,
        scratch_shapes=[pltpu.VMEM((8, 128, 128), F32)],
        compiler_params=params(),
        name="assemble",
    )(z, *ring_gather(summed))
    prob_grad = (prob_total[:, 64:66] / route_probs.astype(F32)).astype(BF)

    block = 512
    down_grad = pl.pallas_call(
        down_kernel,
        out_shape=shape(UNITS, D),
        grid=(D // block,),
        in_specs=[pl.BlockSpec((ROWS, UNITS), lambda i: (0, 0))] * 2
        + [pl.BlockSpec((ROWS, block), lambda i: (0, i))] * 2,
        out_specs=pl.BlockSpec((UNITS, block), lambda i: (0, i)),
        compiler_params=params(),
        name="down_grad",
    )(*hiddens, *rows)
    return (token_grad, prob_grad, down_grad[None])


def solution(mesh):
    return jax.shard_map(
        on_device,
        mesh=mesh,
        in_specs=(
            P("ep", None),
            P("ep", None),
            P("ep", None),
            P("ep", None),
            P("ep", None, "etp"),
            P("ep", None, "etp"),
            P("ep", "etp", None),
        ),
        out_specs=(P("ep", None), P("ep", None), P("ep", "etp", None)),
        check_vma=False,
    )
```

time: 336 us -> 225 us (0.67)
  blocking collectives: 83.8 us -> 18.5 us
  waiting for transfers between devices: 145 us -> 91.4 us
  Pallas kernels: 0 us -> 47.8 us
  starting transfers between devices: 19.8 us -> 56.4 us
  local copies, waits for them, and re-layouts: 34.3 us -> 4.52 us
  matrix products: 24.3 us -> 0 us
  between operations: 14.2 us -> 1.11 us
  other arithmetic: 10.9 us -> 2.47 us
    psum x1 -> x0, waiting for transfers between devices: 67.9 us -> none  [on_device(): lax.psum(partial_value.astype(jnp.bfloat16), 'etp').astype(jnp.float32)]
    ppermute x0 -> x28, waiting for transfers between devices: none -> 60.7 us  [the longest x16 33.1 us: to_right(): return lax.ppermute(x, 'etp', RIGHT)]
    pallas_call x0 -> x9, Pallas kernels: none -> 47.8 us  [the longest x2 18.5 us: on_device(): pl.pallas_call(expert_kernel, out_shape=[shape(128, PACK)] * 8 + [shape(R...]
    all_to_all x2 -> x1, blocking collectives: 65.6 us -> 18.5 us  [exchange(): return lax.all_to_all(x, 'ep', split_axis=0, concat_axis=0, tiled=True)]
    all_to_all x3, waiting for transfers between devices: 77.3 us -> 30.7 us  [exchange(): return lax.all_to_all(x, 'ep', split_axis=0, concat_axis=0, tiled=True)]
    ppermute x0 -> x28, starting transfers between devices: none -> 40.3 us  [the longest x12 35.5 us: to_left(): return lax.ppermute(x, 'etp', LEFT)]
    gather x5 -> x0, local copies, waits for them, and re-layouts: 31.6 us -> none  [the longest x1 9.22 us: on_device(): tokens[token_of]]
    dot_general x6 -> x0, matrix products: 24.3 us -> none  [the longest x3 11.7 us: contract_last(): lax.dot_general(left, right, (((1,), (1,)), ((), ())), preferred_element_...]
  transfers between devices with their start and end apart: 4 -> 31, of which waited for: 3 -> 17; matrix products, arithmetic and copies ran while one was open for 12% -> 1% of each run, Pallas kernels for 0% -> 17%
where the time goes in v1:
time: 225 us; the launch traced here: 222 us
  waiting for transfers between devices  91.4 us (41%)
  starting transfers between devices  56.4 us (25%)
  Pallas kernels  47.8 us (21%)
  blocking collectives  18.5 us (8%)
  local copies, waits for them, and re-layouts  4.52 us (2%)
  other arithmetic  2.47 us (1%)
    ppermute x12, starting transfers between devices, to_left(): return lax.ppermute(x, 'etp', LEFT)  35.5 us
    ppermute x16, waiting for transfers between devices, to_right(): return lax.ppermute(x, 'etp', RIGHT)  33.1 us
    all_to_all x3, waiting for transfers between devices, exchange(): return lax.all_to_all(x, 'ep', split_axis=0, concat_axis=0, tiled=True)  30.7 us
    ppermute x12, waiting for transfers between devices, to_left(): return lax.ppermute(x, 'etp', LEFT)  27.6 us
    all_to_all x1, blocking collectives, exchange(): return lax.all_to_all(x, 'ep', split_axis=0, concat_axis=0, tiled=True)  18.5 us
    pallas_call x2, Pallas kernels, on_device(): pl.pallas_call(expert_kernel, out_shape=[shape(128, PACK)] * 8 + [shape(R...  18.5 us
    all_to_all x3, starting transfers between devices, exchange(): return lax.all_to_all(x, 'ep', split_axis=0, concat_axis=0, tiled=True)  16 us
    pallas_call x1, Pallas kernels, on_device(): pl.pallas_call(functools.partial(gate_up_kernel, OFFSETS), out_shape=[sha...  8.47 us
  transfers between devices with their start and end apart: 31, of which 17 were waited for; matrix products, arithmetic and copies ran while one was open for 1% of the time, Pallas kernels for 17%

profile of v1, /device:TPU:32, one launch (start us, length us, event | category | flops | bytes accessed | tf_op | source)
XLA Modules:
  0.0 222.3 jit_solution(9992660208950818520)
XLA Ops:
  3.0 7.3 %all-to-all-start.1 = ((bf16[32,8,896]{2,1,0:T(8,128)(2,1)}), bf16[32,8,896]{2,1,0:T(8,128)(2,1)S(1)}, u32[]{:S(2)}, u32[]{:S(2)}) async-start(bf16[32,8,896]{2,1,0:T(8,128)(2,1)} %bitcast.34), calls=%async_computation.1 | async-start | bytes 917504 | tf_op jit(solution)/shard_map/all_to_all | solution.py:271
  10.4 3.9 %send_grads.1 = (bf16[256,3584]{1,0:T(8,128)(2,1)}, bf16[256,3584]{1,0:T(8,128)(2,1)}) custom-call(s32[2,128]{1,0:T(2,128)} %bitcast.39, bf16[2,128]{1,0:T(2,128)(2,1)} %bitcast.41, bf16[128,3584]{1,0:T(8,128)(2,1)} %grad_ref.1), custom_call_target="tpu_custom_call" | custom-call | tf_op jit(solution)/shard_map/send_grads/pallas_call | solution.py:295
  14.2 6.7 %all-to-all-done.1 = bf16[32,8,896]{2,1,0:T(8,128)(2,1)S(1)} async-done(((bf16[32,8,896]{2,1,0:T(8,128)(2,1)}), bf16[32,8,896]{2,1,0:T(8,128)(2,1)S(1)}, u32[]{:S(2)}, u32[]{:S(2)}) %all-to-all-start.1) | async-done | bytes 458784 | tf_op jit(solution)/shard_map/all_to_all | solution.py:271
  20.9 4.0 %all-to-all-start = ((bf16[32,8,3584]{2,1,0:T(8,128)(2,1)}), bf16[32,8,3584]{2,1,0:T(8,128)(2,1)S(1)}, u32[]{:S(2)}, u32[]{:S(2)}) async-start(bf16[32,8,3584]{2,1,0:T(8,128)(2,1)} %bitcast.33), calls=%async_computation | async-start | bytes 3670016 | tf_op jit(solution)/shard_map/all_to_all | solution.py:271
  26.9 24.0 %all-to-all-done = bf16[32,8,3584]{2,1,0:T(8,128)(2,1)S(1)} async-done(((bf16[32,8,3584]{2,1,0:T(8,128)(2,1)}), bf16[32,8,3584]{2,1,0:T(8,128)(2,1)S(1)}, u32[]{:S(2)}, u32[]{:S(2)}) %all-to-all-start) | async-done | bytes 1835040 | tf_op jit(solution)/shard_map/all_to_all | solution.py:271
  50.9 4.7 %all-to-all-start.2 = ((bf16[32,8,3584]{2,1,0:T(8,128)(2,1)}), bf16[32,8,3584]{2,1,0:T(8,128)(2,1)}, u32[]{:S(2)}, u32[]{:S(2)}) async-start(bf16[32,8,3584]{2,1,0:T(8,128)(2,1)} %bitcast.32), calls=%async_computation.2 | async-start | bytes 3670016 | tf_op jit(solution)/shard_map/all_to_all | solution.py:271
  57.8 10.7 %collective-permute-done.1.refs_2_ = bf16[256,896]{1,0:T(8,128)(2,1)S(1)} collective-permute-done((bf16[256,896]{1,0:T(8,128)(2,1)S(1)}, bf16[256,896]{1,0:T(8,128)(2,1)S(1)}, u32[]{:S(2)}, u32[]{:S(2)}) %collective-permute-start.1) | collective-permute-done | bytes 458784 | tf_op jit(solution)/shard_map/ppermute | solution.py:241
  68.5 3.3 %collective-permute-start.3 = (bf16[256,896]{1,0:T(8,128)(2,1)S(1)}, bf16[256,896]{1,0:T(8,128)(2,1)S(1)}, u32[]{:S(2)}, u32[]{:S(2)}) collective-permute-start(bf16[256,896]{1,0:T(8,128)(2,1)S(1)} %collective-permute-done.1.refs_2_), channel_id=1, source_target_pairs={{0,7},{1,0},{2,1},{3,2},{4,3},{5,4},{6,5},{7,6},{8,15},{9,8},{10,9... | collective-permute-start | bytes 1376264 | tf_op jit(solution)/shard_map/ppermute | solution.py:241
  72.2 8.7 %collective-permute-done.3.refs_4_ = bf16[256,896]{1,0:T(8,128)(2,1)S(1)} collective-permute-done((bf16[256,896]{1,0:T(8,128)(2,1)S(1)}, bf16[256,896]{1,0:T(8,128)(2,1)S(1)}, u32[]{:S(2)}, u32[]{:S(2)}) %collective-permute-start.3) | collective-permute-done | bytes 458784 | tf_op jit(solution)/shard_map/ppermute | solution.py:241
  81.0 3.8 %collective-permute-start.5 = (bf16[256,896]{1,0:T(8,128)(2,1)S(1)}, bf16[256,896]{1,0:T(8,128)(2,1)S(1)}, u32[]{:S(2)}, u32[]{:S(2)}) collective-permute-start(bf16[256,896]{1,0:T(8,128)(2,1)S(1)} %collective-permute-done.3.refs_4_), channel_id=1, source_target_pairs={{0,7},{1,0},{2,1},{3,2},{4,3},{5,4},{6,5},{7,6},{8,15},{9,8},{10,9... | collective-permute-start | bytes 1376264 | tf_op jit(solution)/shard_map/ppermute | solution.py:241
  85.2 8.2 %collective-permute-done.5.refs_6_ = bf16[256,896]{1,0:T(8,128)(2,1)S(1)} collective-permute-done((bf16[256,896]{1,0:T(8,128)(2,1)S(1)}, bf16[256,896]{1,0:T(8,128)(2,1)S(1)}, u32[]{:S(2)}, u32[]{:S(2)}) %collective-permute-start.5) | collective-permute-done | bytes 458784 | tf_op jit(solution)/shard_map/ppermute | solution.py:241
  93.4 3.9 %collective-permute-done.6.refs_7_ = bf16[256,896]{1,0:T(8,128)(2,1)S(1)} collective-permute-done((bf16[256,896]{1,0:T(8,128)(2,1)S(1)}, bf16[256,896]{1,0:T(8,128)(2,1)S(1)}, u32[]{:S(2)}, u32[]{:S(2)}) %collective-permute-start.6) | collective-permute-done | bytes 458784 | tf_op jit(solution)/shard_map/ppermute | solution.py:237
  98.1 8.5 %gate_up.1 = (f32[256,400]{1,0:T(8,128)}, f32[256,400]{1,0:T(8,128)}, f32[256,400]{1,0:T(8,128)}, f32[256,400]{1,0:T(8,128)}) custom-call(s32[1]{0:T(128)} %bitcast.z_ref, bf16[256,896]{1,0:T(8,128)(2,1)} %bitcast.37, bf16[256,896]{1,0:T(8,128)(2,1)} %copy-done.2, bf16[256,896]{1,0:T(8,128)(2,1)} %copy-done.3, bf16[256,896]{1,0:T(8,128)(2,1)} %copy-done.4, ...), custom_call_target="tpu_custom_call" | custom-call | tf_op jit(solution)/shard_map/gate_up/pallas_call | solution.py:305
  106.6 9.3 %expert.2 = (bf16[128,896]{1,0:T(8,128)(2,1)}, bf16[128,896]{1,0:T(8,128)(2,1)}, bf16[128,896]{1,0:T(8,128)(2,1)}, bf16[128,896]{1,0:T(8,128)(2,1)}, bf16[128,89...) custom-call(s32[1]{0:T(128)} %bitcast.z_ref, ...), custom_call_target="tpu_custom_call" | custom-call | tf_op jit(solution)/shard_map/expert/pallas_call | solution.py:324
  115.9 3.0 %collective-permute-start.11 = (bf16[128,896]{1,0:T(8,128)(2,1)}, bf16[128,896]{1,0:T(8,128)(2,1)S(1)}, u32[]{:S(2)}, u32[]{:S(2)}) collective-permute-start(bf16[128,896]{1,0:T(8,128)(2,1)} %get-tuple-element.39), channel_id=1, source_target_pairs={{0,7},{1,0},{2,1},{3,2},{4,3},{5,4},{6,5},{7,6},{8,15},{9,8},{10,9... | collective-permute-start | bytes 688136 | tf_op jit(solution)/shard_map/ppermute | solution.py:241
  119.0 9.3 %expert.3 = (bf16[128,896]{1,0:T(8,128)(2,1)}, bf16[128,896]{1,0:T(8,128)(2,1)}, bf16[128,896]{1,0:T(8,128)(2,1)}, bf16[128,896]{1,0:T(8,128)(2,1)}, bf16[128,89...) custom-call(s32[1]{0:T(128)} %bitcast.z_ref, ...), custom_call_target="tpu_custom_call" | custom-call | tf_op jit(solution)/shard_map/expert/pallas_call | solution.py:324
  128.4 3.2 %collective-permute-start.18 = (bf16[128,896]{1,0:T(8,128)(2,1)}, bf16[128,896]{1,0:T(8,128)(2,1)S(1)}, u32[]{:S(2)}, u32[]{:S(2)}) collective-permute-start(bf16[128,896]{1,0:T(8,128)(2,1)} %get-tuple-element.50), channel_id=1, source_target_pairs={{0,7},{1,0},{2,1},{3,2},{4,3},{5,4},{6,5},{7,6},{8,15},{9,8},{10,9... | collective-permute-start | bytes 688136 | tf_op jit(solution)/shard_map/ppermute | solution.py:241
  132.1 3.2 %collective-permute-start.12 = (bf16[128,896]{1,0:T(8,128)(2,1)S(1)}, bf16[128,896]{1,0:T(8,128)(2,1)S(1)}, u32[]{:S(2)}, u32[]{:S(2)}) collective-permute-start(bf16[128,896]{1,0:T(8,128)(2,1)S(1)} %add_convert_fusion.6), channel_id=1, source_target_pairs={{0,7},{1,0},{2,1},{3,2},{4,3},{5,4},{6,5},{7,6},{8,15},{9,8},{10,9... | collective-permute-start | bytes 688136 | tf_op jit(solution)/shard_map/ppermute | solution.py:241
  139.6 3.0 %collective-permute-start.19 = (bf16[128,896]{1,0:T(8,128)(2,1)S(1)}, bf16[128,896]{1,0:T(8,128)(2,1)S(1)}, u32[]{:S(2)}, u32[]{:S(2)}) collective-permute-start(bf16[128,896]{1,0:T(8,128)(2,1)S(1)} %add_convert_fusion.1), channel_id=1, source_target_pairs={{0,7},{1,0},{2,1},{3,2},{4,3},{5,4},{6,5},{7,6},{8,15},{9,8},{10,9... | collective-permute-start | bytes 688136 | tf_op jit(solution)/shard_map/ppermute | solution.py:241
  142.9 3.3 %collective-permute-start.13 = (bf16[128,896]{1,0:T(8,128)(2,1)S(1)}, bf16[128,896]{1,0:T(8,128)(2,1)S(1)}, u32[]{:S(2)}, u32[]{:S(2)}) collective-permute-start(bf16[128,896]{1,0:T(8,128)(2,1)S(1)} %add_convert_fusion.5), channel_id=1, source_target_pairs={{0,7},{1,0},{2,1},{3,2},{4,3},{5,4},{6,5},{7,6},{8,15},{9,8},{10,9... | collective-permute-start | bytes 688136 | tf_op jit(solution)/shard_map/ppermute | solution.py:241
  148.3 3.1 %collective-permute-start.20 = (bf16[128,896]{1,0:T(8,128)(2,1)S(1)}, bf16[128,896]{1,0:T(8,128)(2,1)S(1)}, u32[]{:S(2)}, u32[]{:S(2)}) collective-permute-start(bf16[128,896]{1,0:T(8,128)(2,1)S(1)} %add_convert_fusion), channel_id=1, source_target_pairs={{0,7},{1,0},{2,1},{3,2},{4,3},{5,4},{6,5},{7,6},{8,15},{9,8},{10,9... | collective-permute-start | bytes 688136 | tf_op jit(solution)/shard_map/ppermute | solution.py:241
  153.2 4.8 %collective-permute-done.16 = bf16[128,896]{1,0:T(8,128)(2,1)S(1)} collective-permute-done((bf16[128,896]{1,0:T(8,128)(2,1)S(1)}, bf16[128,896]{1,0:T(8,128)(2,1)S(1)}, u32[]{:S(2)}, u32[]{:S(2)}) %collective-permute-start.16) | collective-permute-done | bytes 229408 | tf_op jit(solution)/shard_map/ppermute | solution.py:237
  158.1 3.5 %collective-permute-done.10.refs_1_ = bf16[128,896]{1,0:T(8,128)(2,1)S(1)} collective-permute-done((bf16[128,896]{1,0:T(8,128)(2,1)S(1)}, bf16[128,896]{1,0:T(8,128)(2,1)S(1)}, u32[]{:S(2)}, u32[]{:S(2)}) %collective-permute-start.10) | collective-permute-done | bytes 229408 | tf_op jit(solution)/shard_map/ppermute | solution.py:237
  161.6 3.6 %collective-permute-done.17.refs_4_ = bf16[128,896]{1,0:T(8,128)(2,1)S(1)} collective-permute-done((bf16[128,896]{1,0:T(8,128)(2,1)S(1)}, bf16[128,896]{1,0:T(8,128)(2,1)S(1)}, u32[]{:S(2)}, u32[]{:S(2)}) %collective-permute-start.17) | collective-permute-done | bytes 229408 | tf_op jit(solution)/shard_map/ppermute | solution.py:237
  168.4 18.5 %all_to_all.20 = bf16[32,8,1024]{2,1,0:T(8,128)(2,1)} all-to-all(bf16[32,8,1024]{2,1,0:T(8,128)(2,1)} %bitcast.31), channel_id=1, replica_groups=mesh['ep'=32,'etp'=8] {'ep'}, dimensions={0} | all-to-all | bytes 1048576 | tf_op jit(solution)/shard_map/all_to_all | solution.py:271
  189.3 3.2 %collective-permute-start.22 = (bf16[128,512]{1,0:T(8,128)(2,1)}, bf16[128,512]{1,0:T(8,128)(2,1)S(1)}, u32[]{:S(2)}, u32[]{:S(2)}) collective-permute-start(bf16[128,512]{1,0:T(8,128)(2,1)} %token_sum.1.refs_0_), channel_id=1, source_target_pairs={{0,7},{1,0},{2,1},{3,2},{4,3},{5,4},{6,5},{7,6},{8,15},{9,8},{10,9... | collective-permute-start | bytes 393224 | tf_op jit(solution)/shard_map/ppermute | solution.py:241
  192.5 4.5 %collective-permute-done.21.refs_1_ = bf16[128,512]{1,0:T(8,128)(2,1)S(1)} collective-permute-done((bf16[128,512]{1,0:T(8,128)(2,1)}, bf16[128,512]{1,0:T(8,128)(2,1)S(1)}, u32[]{:S(2)}, u32[]{:S(2)}) %collective-permute-start.21) | collective-permute-done | bytes 131104 | tf_op jit(solution)/shard_map/ppermute | solution.py:237
  197.1 3.1 %collective-permute-start.24 = (bf16[128,512]{1,0:T(8,128)(2,1)S(1)}, bf16[128,512]{1,0:T(8,128)(2,1)S(1)}, u32[]{:S(2)}, u32[]{:S(2)}) collective-permute-start(bf16[128,512]{1,0:T(8,128)(2,1)S(1)} %collective-permute-done.22.refs_2_), channel_id=1, source_target_pairs={{0,7},{1,0},{2,1},{3,2},{4,3},{5,4},{6,5},{7,6},{8,15},{9,8},{10,9... | collective-permute-start | bytes 393224 | tf_op jit(solution)/shard_map/ppermute | solution.py:241
  200.2 3.4 %collective-permute-done.23.refs_3_ = bf16[128,512]{1,0:T(8,128)(2,1)S(1)} collective-permute-done((bf16[128,512]{1,0:T(8,128)(2,1)S(1)}, bf16[128,512]{1,0:T(8,128)(2,1)S(1)}, u32[]{:S(2)}, u32[]{:S(2)}) %collective-permute-start.23) | collective-permute-done | bytes 131104 | tf_op jit(solution)/shard_map/ppermute | solution.py:237
  203.6 3.0 %collective-permute-start.26 = (bf16[128,512]{1,0:T(8,128)(2,1)S(1)}, bf16[128,512]{1,0:T(8,128)(2,1)S(1)}, u32[]{:S(2)}, u32[]{:S(2)}) collective-permute-start(bf16[128,512]{1,0:T(8,128)(2,1)S(1)} %collective-permute-done.24.refs_4_), channel_id=1, source_target_pairs={{0,7},{1,0},{2,1},{3,2},{4,3},{5,4},{6,5},{7,6},{8,15},{9,8},{10,9... | collective-permute-start | bytes 393224 | tf_op jit(solution)/shard_map/ppermute | solution.py:241
  206.6 2.8 %collective-permute-done.25.refs_5_ = bf16[128,512]{1,0:T(8,128)(2,1)S(1)} collective-permute-done((bf16[128,512]{1,0:T(8,128)(2,1)S(1)}, bf16[128,512]{1,0:T(8,128)(2,1)S(1)}, u32[]{:S(2)}, u32[]{:S(2)}) %collective-permute-start.25) | collective-permute-done | bytes 131104 | tf_op jit(solution)/shard_map/ppermute | solution.py:237
  209.5 7.3 %down_grad.1 = bf16[400,3584]{1,0:T(8,128)(2,1)} custom-call(bf16[256,400]{1,0:T(8,128)(2,1)} %get-tuple-element.57.hid0, bf16[256,400]{1,0:T(8,128)(2,1)} %get-tuple-element.58.hid1, bf16[256,3584]{1,0:T(8,128)(2,1)} %bitcast.26, bf16[256,3584]{1,0:T(8,128)(2,1)} %bitcast.15.rows_hbm.rows1), custom_call_target="tpu_custom_call" | custom-call | tf_op jit(solution)/shard_map/down_grad/pallas_call | solution.py:373
  (113 shorter events, 28.3 us)
Async XLA Ops:
  3.0 17.9 %all-to-all-start.1 = ((bf16[32,8,896]{2,1,0:T(8,128)(2,1)}), bf16[32,8,896]{2,1,0:T(8,128)(2,1)S(1)}, u32[]{:S(2)}, u32[]{:S(2)}) async-start(bf16[32,8,896]{2,1,0:T(8,128)(2,1)} %bitcast.34), calls=%async_computation.1 | async-start | bytes 917504 | tf_op jit(solution)/shard_map/all_to_all | solution.py:271
  20.9 30.0 %all-to-all-start = ((bf16[32,8,3584]{2,1,0:T(8,128)(2,1)}), bf16[32,8,3584]{2,1,0:T(8,128)(2,1)S(1)}, u32[]{:S(2)}, u32[]{:S(2)}) async-start(bf16[32,8,3584]{2,1,0:T(8,128)(2,1)} %bitcast.33), calls=%async_computation | async-start | bytes 3670016 | tf_op jit(solution)/shard_map/all_to_all | solution.py:271
  24.9 31.0 %collective-permute-start = (bf16[256,896]{1,0:T(8,128)(2,1)S(1)}, bf16[256,896]{1,0:T(8,128)(2,1)S(1)}, u32[]{:S(2)}, u32[]{:S(2)}) collective-permute-start(bf16[256,896]{1,0:T(8,128)(2,1)S(1)} %bitcast.35), channel_id=1, source_target_pairs={{0,1},{1,2},{2,3},{3,4},{4,5},{5,6},{6,7},{7,0},{8,9},{9,10},{10,1... | collective-permute-start | bytes 1376264 | tf_op jit(solution)/shard_map/ppermute | solution.py:237
  50.9 55.6 %copy-start = (bf16[32,8,3584]{2,1,0:T(8,128)(2,1)}, bf16[32,8,3584]{2,1,0:T(8,128)(2,1)S(1)}, u32[]{:S(2)}) copy-start(bf16[32,8,3584]{2,1,0:T(8,128)(2,1)S(1)} %all-to-all-done) | copy-start | bytes 5505028
  50.9 68.0 %all-to-all-start.2 = ((bf16[32,8,3584]{2,1,0:T(8,128)(2,1)}), bf16[32,8,3584]{2,1,0:T(8,128)(2,1)}, u32[]{:S(2)}, u32[]{:S(2)}) async-start(bf16[32,8,3584]{2,1,0:T(8,128)(2,1)} %bitcast.32), calls=%async_computation.2 | async-start | bytes 3670016 | tf_op jit(solution)/shard_map/all_to_all | solution.py:271
  55.7 12.8 %collective-permute-start.1 = (bf16[256,896]{1,0:T(8,128)(2,1)S(1)}, bf16[256,896]{1,0:T(8,128)(2,1)S(1)}, u32[]{:S(2)}, u32[]{:S(2)}) collective-permute-start(bf16[256,896]{1,0:T(8,128)(2,1)S(1)} %bitcast.36), channel_id=1, source_target_pairs={{0,7},{1,0},{2,1},{3,2},{4,3},{5,4},{6,5},{7,6},{8,15},{9,8},{10,9... | collective-permute-start | bytes 1376264 | tf_op jit(solution)/shard_map/ppermute | solution.py:241
  55.9 16.4 %collective-permute-start.2 = (bf16[256,896]{1,0:T(8,128)(2,1)S(1)}, bf16[256,896]{1,0:T(8,128)(2,1)S(1)}, u32[]{:S(2)}, u32[]{:S(2)}) collective-permute-start(bf16[256,896]{1,0:T(8,128)(2,1)S(1)} %collective-permute-done.refs_1_), channel_id=1, source_target_pairs={{0,1},{1,2},{2,3},{3,4},{4,5},{5,6},{6,7},{7,0},{8,9},{9,10},{10,1... | collective-permute-start | bytes 1376264 | tf_op jit(solution)/shard_map/ppermute | solution.py:237
  68.5 12.5 %collective-permute-start.3 = (bf16[256,896]{1,0:T(8,128)(2,1)S(1)}, bf16[256,896]{1,0:T(8,128)(2,1)S(1)}, u32[]{:S(2)}, u32[]{:S(2)}) collective-permute-start(bf16[256,896]{1,0:T(8,128)(2,1)S(1)} %collective-permute-done.1.refs_2_), channel_id=1, source_target_pairs={{0,7},{1,0},{2,1},{3,2},{4,3},{5,4},{6,5},{7,6},{8,15},{9,8},{10,9... | collective-permute-start | bytes 1376264 | tf_op jit(solution)/shard_map/ppermute | solution.py:241
  72.2 13.0 %collective-permute-start.4 = (bf16[256,896]{1,0:T(8,128)(2,1)S(1)}, bf16[256,896]{1,0:T(8,128)(2,1)S(1)}, u32[]{:S(2)}, u32[]{:S(2)}) collective-permute-start(bf16[256,896]{1,0:T(8,128)(2,1)S(1)} %collective-permute-done.2.refs_3_), channel_id=1, source_target_pairs={{0,1},{1,2},{2,3},{3,4},{4,5},{5,6},{6,7},{7,0},{8,9},{9,10},{10,1... | collective-permute-start | bytes 1376264 | tf_op jit(solution)/shard_map/ppermute | solution.py:237
  81.0 12.4 %collective-permute-start.5 = (bf16[256,896]{1,0:T(8,128)(2,1)S(1)}, bf16[256,896]{1,0:T(8,128)(2,1)S(1)}, u32[]{:S(2)}, u32[]{:S(2)}) collective-permute-start(bf16[256,896]{1,0:T(8,128)(2,1)S(1)} %collective-permute-done.3.refs_4_), channel_id=1, source_target_pairs={{0,7},{1,0},{2,1},{3,2},{4,3},{5,4},{6,5},{7,6},{8,15},{9,8},{10,9... | collective-permute-start | bytes 1376264 | tf_op jit(solution)/shard_map/ppermute | solution.py:241
  85.2 12.1 %collective-permute-start.6 = (bf16[256,896]{1,0:T(8,128)(2,1)S(1)}, bf16[256,896]{1,0:T(8,128)(2,1)S(1)}, u32[]{:S(2)}, u32[]{:S(2)}) collective-permute-start(bf16[256,896]{1,0:T(8,128)(2,1)S(1)} %collective-permute-done.4.refs_5_), channel_id=1, source_target_pairs={{0,1},{1,2},{2,3},{3,4},{4,5},{5,6},{6,7},{7,0},{8,9},{9,10},{10,1... | collective-permute-start | bytes 1376264 | tf_op jit(solution)/shard_map/ppermute | solution.py:237
  115.9 15.8 %collective-permute-start.7 = (bf16[128,896]{1,0:T(8,128)(2,1)}, bf16[128,896]{1,0:T(8,128)(2,1)S(1)}, u32[]{:S(2)}, u32[]{:S(2)}) collective-permute-start(bf16[128,896]{1,0:T(8,128)(2,1)} %get-tuple-element.35), channel_id=1, source_target_pairs={{0,1},{1,2},{2,3},{3,4},{4,5},{5,6},{6,7},{7,0},{8,9},{9,10},{10,1... | collective-permute-start | bytes 688136 | tf_op jit(solution)/shard_map/ppermute | solution.py:237
  115.9 16.1 %collective-permute-start.11 = (bf16[128,896]{1,0:T(8,128)(2,1)}, bf16[128,896]{1,0:T(8,128)(2,1)S(1)}, u32[]{:S(2)}, u32[]{:S(2)}) collective-permute-start(bf16[128,896]{1,0:T(8,128)(2,1)} %get-tuple-element.39), channel_id=1, source_target_pairs={{0,7},{1,0},{2,1},{3,2},{4,3},{5,4},{6,5},{7,6},{8,15},{9,8},{10,9... | collective-permute-start | bytes 688136 | tf_op jit(solution)/shard_map/ppermute | solution.py:241
  128.3 9.3 %collective-permute-start.14 = (bf16[128,896]{1,0:T(8,128)(2,1)}, bf16[128,896]{1,0:T(8,128)(2,1)S(1)}, u32[]{:S(2)}, u32[]{:S(2)}) collective-permute-start(bf16[128,896]{1,0:T(8,128)(2,1)} %get-tuple-element.46), channel_id=1, source_target_pairs={{0,1},{1,2},{2,3},{3,4},{4,5},{5,6},{6,7},{7,0},{8,9},{9,10},{10,1... | collective-permute-start | bytes 688136 | tf_op jit(solution)/shard_map/ppermute | solution.py:237
  128.4 10.3 %collective-permute-start.18 = (bf16[128,896]{1,0:T(8,128)(2,1)}, bf16[128,896]{1,0:T(8,128)(2,1)S(1)}, u32[]{:S(2)}, u32[]{:S(2)}) collective-permute-start(bf16[128,896]{1,0:T(8,128)(2,1)} %get-tuple-element.50), channel_id=1, source_target_pairs={{0,7},{1,0},{2,1},{3,2},{4,3},{5,4},{6,5},{7,6},{8,15},{9,8},{10,9... | collective-permute-start | bytes 688136 | tf_op jit(solution)/shard_map/ppermute | solution.py:241
  131.7 11.0 %collective-permute-start.8 = (bf16[128,896]{1,0:T(8,128)(2,1)S(1)}, bf16[128,896]{1,0:T(8,128)(2,1)S(1)}, u32[]{:S(2)}, u32[]{:S(2)}) collective-permute-start(bf16[128,896]{1,0:T(8,128)(2,1)S(1)} %add_convert_fusion.9), channel_id=1, source_target_pairs={{0,1},{1,2},{2,3},{3,4},{4,5},{5,6},{6,7},{7,0},{8,9},{9,10},{10,1... | collective-permute-start | bytes 688136 | tf_op jit(solution)/shard_map/ppermute | solution.py:237
  132.1 10.7 %collective-permute-start.12 = (bf16[128,896]{1,0:T(8,128)(2,1)S(1)}, bf16[128,896]{1,0:T(8,128)(2,1)S(1)}, u32[]{:S(2)}, u32[]{:S(2)}) collective-permute-start(bf16[128,896]{1,0:T(8,128)(2,1)S(1)} %add_convert_fusion.6), channel_id=1, source_target_pairs={{0,7},{1,0},{2,1},{3,2},{4,3},{5,4},{6,5},{7,6},{8,15},{9,8},{10,9... | collective-permute-start | bytes 688136 | tf_op jit(solution)/shard_map/ppermute | solution.py:241
  138.5 9.5 %collective-permute-start.15 = (bf16[128,896]{1,0:T(8,128)(2,1)S(1)}, bf16[128,896]{1,0:T(8,128)(2,1)S(1)}, u32[]{:S(2)}, u32[]{:S(2)}) collective-permute-start(bf16[128,896]{1,0:T(8,128)(2,1)S(1)} %add_convert_fusion.4), channel_id=1, source_target_pairs={{0,1},{1,2},{2,3},{3,4},{4,5},{5,6},{6,7},{7,0},{8,9},{9,10},{10,1... | collective-permute-start | bytes 688136 | tf_op jit(solution)/shard_map/ppermute | solution.py:237
  139.6 8.6 %collective-permute-start.19 = (bf16[128,896]{1,0:T(8,128)(2,1)S(1)}, bf16[128,896]{1,0:T(8,128)(2,1)S(1)}, u32[]{:S(2)}, u32[]{:S(2)}) collective-permute-start(bf16[128,896]{1,0:T(8,128)(2,1)S(1)} %add_convert_fusion.1), channel_id=1, source_target_pairs={{0,7},{1,0},{2,1},{3,2},{4,3},{5,4},{6,5},{7,6},{8,15},{9,8},{10,9... | collective-permute-start | bytes 688136 | tf_op jit(solution)/shard_map/ppermute | solution.py:241
  142.7 10.3 %collective-permute-start.9 = (bf16[128,896]{1,0:T(8,128)(2,1)S(1)}, bf16[128,896]{1,0:T(8,128)(2,1)S(1)}, u32[]{:S(2)}, u32[]{:S(2)}) collective-permute-start(bf16[128,896]{1,0:T(8,128)(2,1)S(1)} %add_convert_fusion.8), channel_id=1, source_target_pairs={{0,1},{1,2},{2,3},{3,4},{4,5},{5,6},{6,7},{7,0},{8,9},{9,10},{10,1... | collective-permute-start | bytes 688136 | tf_op jit(solution)/shard_map/ppermute | solution.py:237
  142.9 15.2 %collective-permute-start.13 = (bf16[128,896]{1,0:T(8,128)(2,1)S(1)}, bf16[128,896]{1,0:T(8,128)(2,1)S(1)}, u32[]{:S(2)}, u32[]{:S(2)}) collective-permute-start(bf16[128,896]{1,0:T(8,128)(2,1)S(1)} %add_convert_fusion.5), channel_id=1, source_target_pairs={{0,7},{1,0},{2,1},{3,2},{4,3},{5,4},{6,5},{7,6},{8,15},{9,8},{10,9... | collective-permute-start | bytes 688136 | tf_op jit(solution)/shard_map/ppermute | solution.py:241
  148.1 9.8 %collective-permute-start.16 = (bf16[128,896]{1,0:T(8,128)(2,1)S(1)}, bf16[128,896]{1,0:T(8,128)(2,1)S(1)}, u32[]{:S(2)}, u32[]{:S(2)}) collective-permute-start(bf16[128,896]{1,0:T(8,128)(2,1)S(1)} %add_convert_fusion.3), channel_id=1, source_target_pairs={{0,1},{1,2},{2,3},{3,4},{4,5},{5,6},{6,7},{7,0},{8,9},{9,10},{10,1... | collective-permute-start | bytes 688136 | tf_op jit(solution)/shard_map/ppermute | solution.py:237
  148.3 9.8 %collective-permute-start.20 = (bf16[128,896]{1,0:T(8,128)(2,1)S(1)}, bf16[128,896]{1,0:T(8,128)(2,1)S(1)}, u32[]{:S(2)}, u32[]{:S(2)}) collective-permute-start(bf16[128,896]{1,0:T(8,128)(2,1)S(1)} %add_convert_fusion), channel_id=1, source_target_pairs={{0,7},{1,0},{2,1},{3,2},{4,3},{5,4},{6,5},{7,6},{8,15},{9,8},{10,9... | collective-permute-start | bytes 688136 | tf_op jit(solution)/shard_map/ppermute | solution.py:241
  153.1 8.5 %collective-permute-start.10 = (bf16[128,896]{1,0:T(8,128)(2,1)S(1)}, bf16[128,896]{1,0:T(8,128)(2,1)S(1)}, u32[]{:S(2)}, u32[]{:S(2)}) collective-permute-start(bf16[128,896]{1,0:T(8,128)(2,1)S(1)} %add_convert_fusion.7), channel_id=1, source_target_pairs={{0,1},{1,2},{2,3},{3,4},{4,5},{5,6},{6,7},{7,0},{8,9},{9,10},{10,1... | collective-permute-start | bytes 688136 | tf_op jit(solution)/shard_map/ppermute | solution.py:237
  158.0 7.2 %collective-permute-start.17 = (bf16[128,896]{1,0:T(8,128)(2,1)S(1)}, bf16[128,896]{1,0:T(8,128)(2,1)S(1)}, u32[]{:S(2)}, u32[]{:S(2)}) collective-permute-start(bf16[128,896]{1,0:T(8,128)(2,1)S(1)} %add_convert_fusion.2), channel_id=1, source_target_pairs={{0,1},{1,2},{2,3},{3,4},{4,5},{5,6},{6,7},{7,0},{8,9},{9,10},{10,1... | collective-permute-start | bytes 688136 | tf_op jit(solution)/shard_map/ppermute | solution.py:237
  189.3 7.8 %collective-permute-start.21 = (bf16[128,512]{1,0:T(8,128)(2,1)}, bf16[128,512]{1,0:T(8,128)(2,1)S(1)}, u32[]{:S(2)}, u32[]{:S(2)}) collective-permute-start(bf16[128,512]{1,0:T(8,128)(2,1)} %token_sum.1.refs_0_), channel_id=1, source_target_pairs={{0,1},{1,2},{2,3},{3,4},{4,5},{5,6},{6,7},{7,0},{8,9},{9,10},{10,1... | collective-permute-start | bytes 393224 | tf_op jit(solution)/shard_map/ppermute | solution.py:237
  189.3 7.8 %collective-permute-start.22 = (bf16[128,512]{1,0:T(8,128)(2,1)}, bf16[128,512]{1,0:T(8,128)(2,1)S(1)}, u32[]{:S(2)}, u32[]{:S(2)}) collective-permute-start(bf16[128,512]{1,0:T(8,128)(2,1)} %token_sum.1.refs_0_), channel_id=1, source_target_pairs={{0,7},{1,0},{2,1},{3,2},{4,3},{5,4},{6,5},{7,6},{8,15},{9,8},{10,9... | collective-permute-start | bytes 393224 | tf_op jit(solution)/shard_map/ppermute | solution.py:241
  197.1 6.5 %collective-permute-start.23 = (bf16[128,512]{1,0:T(8,128)(2,1)S(1)}, bf16[128,512]{1,0:T(8,128)(2,1)S(1)}, u32[]{:S(2)}, u32[]{:S(2)}) collective-permute-start(bf16[128,512]{1,0:T(8,128)(2,1)S(1)} %collective-permute-done.21.refs_1_), channel_id=1, source_target_pairs={{0,1},{1,2},{2,3},{3,4},{4,5},{5,6},{6,7},{7,0},{8,9},{9,10},{10,1... | collective-permute-start | bytes 393224 | tf_op jit(solution)/shard_map/ppermute | solution.py:237
  197.1 6.5 %collective-permute-start.24 = (bf16[128,512]{1,0:T(8,128)(2,1)S(1)}, bf16[128,512]{1,0:T(8,128)(2,1)S(1)}, u32[]{:S(2)}, u32[]{:S(2)}) collective-permute-start(bf16[128,512]{1,0:T(8,128)(2,1)S(1)} %collective-permute-done.22.refs_2_), channel_id=1, source_target_pairs={{0,7},{1,0},{2,1},{3,2},{4,3},{5,4},{6,5},{7,6},{8,15},{9,8},{10,9... | collective-permute-start | bytes 393224 | tf_op jit(solution)/shard_map/ppermute | solution.py:241
  203.6 5.9 %collective-permute-start.25 = (bf16[128,512]{1,0:T(8,128)(2,1)S(1)}, bf16[128,512]{1,0:T(8,128)(2,1)S(1)}, u32[]{:S(2)}, u32[]{:S(2)}) collective-permute-start(bf16[128,512]{1,0:T(8,128)(2,1)S(1)} %collective-permute-done.23.refs_3_), channel_id=1, source_target_pairs={{0,1},{1,2},{2,3},{3,4},{4,5},{5,6},{6,7},{7,0},{8,9},{9,10},{10,1... | collective-permute-start | bytes 393224 | tf_op jit(solution)/shard_map/ppermute | solution.py:237
  203.6 13.2 %collective-permute-start.26 = (bf16[128,512]{1,0:T(8,128)(2,1)S(1)}, bf16[128,512]{1,0:T(8,128)(2,1)S(1)}, u32[]{:S(2)}, u32[]{:S(2)}) collective-permute-start(bf16[128,512]{1,0:T(8,128)(2,1)S(1)} %collective-permute-done.24.refs_4_), channel_id=1, source_target_pairs={{0,7},{1,0},{2,1},{3,2},{4,3},{5,4},{6,5},{7,6},{8,15},{9,8},{10,9... | collective-permute-start | bytes 393224 | tf_op jit(solution)/shard_map/ppermute | solution.py:241
  209.5 7.4 %collective-permute-start.27 = (bf16[128,512]{1,0:T(8,128)(2,1)S(1)}, bf16[128,512]{1,0:T(8,128)(2,1)S(1)}, u32[]{:S(2)}, u32[]{:S(2)}) collective-permute-start(bf16[128,512]{1,0:T(8,128)(2,1)S(1)} %collective-permute-done.25.refs_5_), channel_id=1, source_target_pairs={{0,1},{1,2},{2,3},{3,4},{4,5},{5,6},{6,7},{7,0},{8,9},{9,10},{10,1... | collective-permute-start | bytes 393224 | tf_op jit(solution)/shard_map/ppermute | solution.py:237
  (28 other events, 413.7 us)
